TPU v7x, 256 devices: a whole 4x4x8 slice. The times are simulated.
256 devices in a mesh: pipe: 16 (over z, core), dp: 16 (over y, x).
Axes of the slice: x: 4, y: 4, z: 8, core: 2. Of those that a mesh axis runs over, the one named last changes fastest.
Arguments:
- saved: bfloat16 [16, 1, 768, 16384], P('pipe', None, None, 'dp'), may hold values from -6 to 6
- grads_in: bfloat16 [16, 768, 16384], P('pipe', None, 'dp'), may hold values from -6 to 6
- gains: bfloat16 [16, 1, 16384], P('pipe', None, 'dp'), may hold values from 0.25 to 1.75
- w_in: bfloat16 [16, 1, 16384, 1024], P('pipe', None, 'dp'), may hold values from -0.1875 to 0.1875
- w_out_t: bfloat16 [16, 1, 16384, 1024], P('pipe', None, 'dp'), may hold values from -0.046875 to 0.046875
- encoder: bfloat16 [16384, 4096], P('dp', 'pipe'), may hold values from -0.046875 to 0.046875
- enc_bias: float32 [4096], P('pipe'), may hold values from -4 to 4
- decoder: bfloat16 [4096, 16384], P('pipe', 'dp'), may hold values from -0.09375 to 0.09375
- transcoder_norm_gain: bfloat16 [16384], P('dp'), may hold values from 0.25 to 1.75
Outputs:
- grads_out: bfloat16 [16, 768, 16384], P('pipe', None, 'dp')
- grad_encoder: float32 [16384, 4096], P('dp', 'pipe')
- grad_decoder: float32 [4096, 16384], P('pipe', 'dp')
- grad_bias: float32 [4096], P('pipe')
All inputs are finite; a program needn't handle non-finite values.
Results may differ from a plain program's by a relative error of at most 0.007.
Values may be sent and summed in bfloat16 or wider, within the bound.
A program may use at most 64 MiB of HBM per device.

v0:
```python
import jax
import jax.numpy as jnp
from jax import lax
from jax.sharding import PartitionSpec as P

MODEL_WIDTH = 16384


def passed_along(array, axis, by):
    peers = lax.axis_size(axis)
    return lax.ppermute(array, axis, [(i, (i + by) % peers) for i in range(peers)])


def from_root(block, axis, source):
    block = jnp.where(lax.axis_index(axis) == source, block, jnp.zeros_like(block))
    return lax.psum(block, axis)


def width_total_sum(values):
    return lax.psum(values, "dp")


def gelu_tanh(v):
    return jax.nn.gelu(v, approximate=True)


def scale_from(squares):
    return lax.rsqrt(squares / MODEL_WIDTH + 1e-05)


def forward_part(first_in, transcoder_norm_gain, encoder, enc_bias):
    residual_float = first_in.astype(jnp.float32)
    inverse_scale = scale_from(
        width_total_sum(jnp.sum(residual_float * residual_float, axis=-1, keepdims=True))
    )
    transcoder_norm = (
        residual_float * inverse_scale * transcoder_norm_gain.astype(jnp.float32)
    ).astype(jnp.bfloat16)
    tpre = (
        width_total_sum(jnp.dot(transcoder_norm, encoder, preferred_element_type=jnp.float32))
        + enc_bias
    )
    return (transcoder_norm, tpre)


def body(saved, grads_in, gains, w_in, w_out_t, encoder, enc_bias, decoder, transcoder_norm_gain):
    output_gradient = grads_in[0]
    residual_float = saved[0, 0].astype(jnp.float32)
    gain = gains[0, 0].astype(jnp.float32)
    inverse_scale = scale_from(
        width_total_sum(jnp.sum(residual_float * residual_float, axis=-1, keepdims=True))
    )
    normalized_input = residual_float * inverse_scale
    partial_value = jnp.dot(output_gradient, w_out_t[0, 0], preferred_element_type=jnp.float32)
    dvalue = width_total_sum(partial_value).astype(jnp.bfloat16)
    dnorm = jnp.dot(dvalue, w_in[0, 0].T, preferred_element_type=jnp.float32)
    upper_gradient = dnorm * gain
    inner_product = (
        width_total_sum(jnp.sum(upper_gradient * normalized_input, axis=-1, keepdims=True))
        / MODEL_WIDTH
    )
    residual_gradient = (
        output_gradient.astype(jnp.float32)
        + inverse_scale * (upper_gradient - normalized_input * inner_product)
    ).astype(jnp.bfloat16)
    output_gradient = passed_along(residual_gradient, "pipe", -1)
    first_in, upstream = (from_root(saved[0, 0], "pipe", 0), from_root(output_gradient, "pipe", 0))
    transcoder_norm, tpre = forward_part(first_in, transcoder_norm_gain, encoder, enc_bias)
    latent = gelu_tanh(tpre).astype(jnp.bfloat16)
    dlat = width_total_sum(jnp.dot(upstream, decoder.T, preferred_element_type=jnp.float32))
    _, gelu_back = jax.vjp(gelu_tanh, tpre)
    dtpre = gelu_back(dlat)[0].astype(jnp.bfloat16)
    grad_encoder = jnp.dot(transcoder_norm.T, dtpre, preferred_element_type=jnp.float32)
    grad_decoder = jnp.dot(latent.T, upstream, preferred_element_type=jnp.float32)
    grad_bias = jnp.sum(dtpre.astype(jnp.float32), axis=0)
    return (output_gradient[None], grad_encoder, grad_decoder, grad_bias)


def solution(mesh):
    in_specs = (
        P("pipe", None, None, "dp"),
        P("pipe", None, "dp"),
        P("pipe", None, "dp"),
        P("pipe", None, "dp", None),
        P("pipe", None, "dp", None),
        P("dp", "pipe"),
        P("pipe"),
        P("pipe", "dp"),
        P("dp"),
    )
    out_specs = (P("pipe", None, "dp"), P("dp", "pipe"), P("pipe", "dp"), P("pipe"))
    return jax.shard_map(body, mesh=mesh, in_specs=in_specs, out_specs=out_specs, check_vma=False)
```

profile of v0, /device:TPU:65, one launch (start us, length us, event | category | flops | bytes accessed | tf_op | source)
XLA Modules:
  0.0 420.5 jit_solution(1374161490819025660)
XLA Ops:
  7.2 0.0 all-reduce.8.cloned.1.call-start
  7.2 1.3 select_bitcast_fusion
  8.5 0.0 all-reduce.10.cloned.1.call-start
  8.6 1.8 fusion.10
  10.4 5.5 %fusion.13 = f32[768,1024]{1,0:T(8,128)} fusion(bf16[1,1,1024,1024]{3,2,1,0:T(8,128)(2,1)} %param.13, bf16[1,768,1024]{2,1,0:T(8,128)(2,1)} %param.10), kind=kOutput, calls=%fused_computation.17 | convolution fusion | flops 1610612736 | bytes 6815744 | tf_op jit(solution)/shard_map/dot_general | solution.py:54
  15.9 87.2 %all-reduce.13 = (bf16[768,1024]{1,0:T(8,128)(2,1)}, f32[768,1]{0,1:T(1,128)S(1)}) all-reduce(f32[768,1024]{1,0:T(8,128)} %fusion.13, f32[768,1]{0,1:T(1,128)S(1)} %broadcast_in_dim.15), channel_id=1, replica_groups=mesh['pipe'=16,'dp'=16] {'dp'}, use_global_device_ids=true, to_apply=%region_2.0 | all-reduce | flops 787200 | bytes 4724736 | tf_op jit(solution)/shard_map/psum | solution.py:20
  103.1 5.5 %fusion.2 = (f32[768]{0:T(1024)S(1)}, f32[768,1024]{1,0:T(8,128)}) fusion(bf16[1,1,768,1024]{3,2,1,0:T(8,128)(2,1)} %param.9, f32[1024]{0:T(1024)S(1)} %bitcast.28, f32[768]{0:T(1024)S(1)} %rsqrt_reduce_fusion.1, bf16[768,1024]{1,0:T(8,128)(2,1)} %get-tuple-element.6, bf16[1,1,1024,1024]{3,2,1,0:T(8,128)(2,1)S(1)} %copy-done), kind=kOutput, calls=%fused_computation.6 | convolution fusion | flops 1614544128 | bytes 8398848 | tf_op jit(solution)/shard_map/dot_general | solution.py:56
  108.6 17.5 %all-reduce.8.cloned.1.call-done = bf16[768,1024]{1,0:T(8,128)(2,1)} async-done(((bf16[768,1024]{1,0:T(8,128)(2,1)}), bf16[768,1024]{1,0:T(8,128)(2,1)}) %all-reduce.8.cloned.1.call-update) | async-done | bytes 1572880 | tf_op jit(solution)/shard_map/psum | solution.py:16
  126.1 1.8 fusion.7
  127.9 34.0 %all-reduce = (f32[768,1]{0,1:T(1,128)S(1)}, f32[768,1]{0,1:T(1,128)S(1)}) all-reduce(f32[768,1]{0,1:T(1,128)S(1)} %broadcast_in_dim.16, f32[768,1]{0,1:T(1,128)S(1)} %broadcast_in_dim.18), channel_id=1, replica_groups=mesh['pipe'=16,'dp'=16] {'dp'}, use_global_device_ids=true, to_apply=%region_4.0 | all-reduce | flops 1536 | bytes 12288 | tf_op jit(solution)/shard_map/psum | solution.py:20
  162.0 3.8 fusion.6
  165.7 6.5 %collective-permute-start = (bf16[768,1024]{1,0:T(8,128)(2,1)S(1)}, bf16[768,1024]{1,0:T(8,128)(2,1)S(1)}, u32[]{:S(2)}, u32[]{:S(2)}) collective-permute-start(bf16[768,1024]{1,0:T(8,128)(2,1)S(1)} %fusion.6), channel_id=1, source_target_pairs={{0,240},{16,0},{32,16},{48,32},{64,48},{80,64},{96,80},{112,96},{1... | collective-permute-start | bytes 4718600 | tf_op jit(solution)/shard_map/ppermute | solution.py:11
  172.2 20.4 %collective-permute-done = bf16[768,1024]{1,0:T(8,128)(2,1)S(1)} collective-permute-done((bf16[768,1024]{1,0:T(8,128)(2,1)S(1)}, bf16[768,1024]{1,0:T(8,128)(2,1)S(1)}, u32[]{:S(2)}, u32[]{:S(2)}) %collective-permute-start) | collective-permute-done | bytes 1572896 | tf_op jit(solution)/shard_map/ppermute | solution.py:11
  192.7 1.1 copy-done.1
  193.8 1.3 broadcast_select_fusion
  195.1 0.0 all-reduce.12.cloned.1.call-start
  195.2 3.0 fusion.26
  198.1 104.0 %all-reduce.10.cloned.1.call-done = bf16[768,1024]{1,0:T(8,128)(2,1)} async-done(((bf16[768,1024]{1,0:T(8,128)(2,1)}), bf16[768,1024]{1,0:T(8,128)(2,1)}) %all-reduce.10.cloned.1.call-update) | async-done | bytes 1572880 | tf_op jit(solution)/shard_map/psum | solution.py:16
  302.1 2.9 fusion.39
  305.0 100.0 %all-reduce.12.cloned.1.call-done = (f32[768,256]{1,0:T(8,128)}, f32[768,256]{1,0:T(8,128)}) async-done(((f32[768,256]{1,0:T(8,128)}, f32[768,256]{1,0:T(8,128)}), (f32[768,256]{1,0:T(8,128)}, f32[768,256]{1,0:T(8,128)})) %all-reduce.12.cloned.1.call-update) | async-done | bytes 1572880 | tf_op jit(solution)/shard_map/psum | solution.py:20
  405.0 2.5 convert_reduce_fusion
  407.6 3.4 fusion.28
  411.0 1.8 fusion.24
  412.8 1.1 copy.21
  (28 shorter events, 0.2 us)
Async XLA Ops:
  7.2 96.0 %copy-start = (bf16[1,1,1024,1024]{3,2,1,0:T(8,128)(2,1)S(1)}, bf16[1,1,1024,1024]{3,2,1,0:T(8,128)(2,1)}, u32[]{:S(2)}) copy-start(bf16[1,1,1024,1024]{3,2,1,0:T(8,128)(2,1)} %param.12) | copy-start | bytes 6291460
  7.2 119.0 %all-reduce.8.cloned.1.call-start = ((), (), s32[]{:S(2)}) async-start(), calls=%async_computation | async-start | bytes 3145728 | tf_op jit(solution)/shard_map/psum | solution.py:16
  8.5 293.6 %all-reduce.10.cloned.1.call-start = ((), (), s32[]{:S(2)}) async-start(), calls=%async_computation.1 | async-start | bytes 3145728 | tf_op jit(solution)/shard_map/psum | solution.py:16
  15.9 87.2 %copy-start.5 = (bf16[1,1,1024]{2,1,0:T(2,128)(2,1)S(1)}, bf16[1,1,1024]{2,1,0:T(2,128)(2,1)}, u32[]{:S(2)}) copy-start(bf16[1,1,1024]{2,1,0:T(2,128)(2,1)} %param.11) | copy-start | bytes 6148
  165.7 29.4 %copy-start.6 = (bf16[1024]{0:T(1024)(128)(2,1)S(1)}, bf16[1024]{0:T(1024)(128)(2,1)}, u32[]{:S(2)}) copy-start(bf16[1024]{0:T(1024)(128)(2,1)} %param.17) | copy-start | bytes 6148
  165.7 29.4 %copy-start.8 = (bf16[1024,256]{1,0:T(8,128)(2,1)S(1)}, bf16[1024,256]{1,0:T(8,128)(2,1)}, u32[]{:S(2)}) copy-start(bf16[1024,256]{1,0:T(8,128)(2,1)} %param.14) | copy-start | bytes 1572868
  165.7 26.9 %collective-permute-start = (bf16[768,1024]{1,0:T(8,128)(2,1)S(1)}, bf16[768,1024]{1,0:T(8,128)(2,1)S(1)}, u32[]{:S(2)}, u32[]{:S(2)}) collective-permute-start(bf16[768,1024]{1,0:T(8,128)(2,1)S(1)} %fusion.6), channel_id=1, source_target_pairs={{0,240},{16,0},{32,16},{48,32},{64,48},{80,64},{96,80},{112,96},{1... | collective-permute-start | bytes 4718600 | tf_op jit(solution)/shard_map/ppermute | solution.py:11
  192.7 1.1 copy-start.1
  195.1 107.1 %copy-start.4 = (bf16[256,1024]{1,0:T(8,128)(2,1)S(1)}, bf16[256,1024]{1,0:T(8,128)(2,1)}, u32[]{:S(2)}) copy-start(bf16[256,1024]{1,0:T(8,128)(2,1)} %param.16) | copy-start | bytes 1572868
  195.1 209.9 %all-reduce.12.cloned.1.call-start = ((), (), s32[]{:S(2)}) async-start(), calls=%async_computation.2 | async-start | bytes 3145728 | tf_op jit(solution)/shard_map/psum | solution.py:20
  198.1 206.9 %copy-start.7 = (f32[256]{0:T(256)S(1)}, f32[256]{0:T(256)}, u32[]{:S(2)}) copy-start(f32[256]{0:T(256)} %param.15) | copy-start | bytes 3076
  407.6 3.4 copy-start.3
  411.0 1.8 copy-start.2
Sparse Core Ops, SparseCore 0:
  10.4 115.7 all-reduce.7
  195.2 106.8 all-reduce.9
  306.0 98.9 all-reduce.11
where the time goes:
time: 423 us; the launch traced here: 420 us
  waiting for transfers between devices  242 us (57%)
  blocking collectives  121 us (29%)
  matrix products  22.1 us (5%)
  between operations  13.9 us (3%)
  other arithmetic  12.5 us (3%)
  starting transfers between devices  6.62 us (2%)
    psum x2, waiting for transfers between devices, from_root(): return lax.psum(block, axis)  122 us
    psum x2, blocking collectives, width_total_sum(): return lax.psum(values, 'dp')  121 us
    psum x1, waiting for transfers between devices, width_total_sum(): return lax.psum(values, 'dp')  100 us
    ppermute x1, waiting for transfers between devices, passed_along(): lax.ppermute(array, axis, [(i, (i + by) % peers) for i in range(peers)])  20.4 us
  transfers between devices with their start and end apart: 4, of which 4 were waited for; matrix products, arithmetic and copies ran while one was open for 4% of the time, Pallas kernels for 0%

commit v1 on v0

v1 whole, which is shorter than its diff:
```python
import functools

import jax
import jax.numpy as jnp
from jax import lax
from jax.experimental import pallas as pl
from jax.experimental.pallas import tpu as pltpu
from jax.sharding import PartitionSpec as P

MESH = pl.DeviceIdType.MESH
BF = jnp.bfloat16
F32 = jnp.float32
MODEL_WIDTH = 16384
T, W, H, L = 768, 1024, 1024, 256
C, TC = 3, 256
Q, QW = 4, 256
DP, PIPE = 16, 16
TS = TC // DP
BLK = 64
HALF = T // 2
NB = HALF // BLK
TN_FIRST = 2
GELU_A = 0.7978845608028654
GELU_B = 0.044715


def dot(a, b, dims=((1,), (0,))):
    return lax.dot_general(a, b, (dims, ((), ())), preferred_element_type=F32)


def row_total(block):
    lanes = block[:, 0:128]
    for j in range(1, block.shape[1] // 128):
        lanes = lanes + block[:, j * 128 : (j + 1) * 128]
    return jnp.sum(lanes.T, axis=0, keepdims=True)


def as_columns(row):
    return jnp.broadcast_to(row, (128, row.shape[1])).T


def kernel(
    gains, bias, tgain, saved, gin, win, wout, enc, dec,
    gout, genc, gdec, gbias,
    x_v, gin_v, win_v, wout_v, enc_v, dec_v,
    dhp, r0, r1, r2, r3, s1, k1, s2, k2, s3, k3, dhf, uf, dx, tn, gt,
    sqb, ipb, rcol, part, rsb, tps, full, ge_v, gd_v,
    load_sem, rs_send, rs_recv, sq_sem, ip_send, ip_recv, tr_send, tr_recv,
    tn_recv, tn_send, tnx_recv, gt_recv, gt_send, gtx_recv, go_send, go_recv, out_sem,
):
    p = lax.axis_index("pipe")
    d = lax.axis_index("dp")
    z, core = p // 2, p % 2
    y, x = d // 4, d % 4
    bits = (((x + 1) // 2) % 2, x // 2, ((y + 1) // 2) % 2, y // 2)
    peers = (
        y * 4 + (x + 1 - 2 * (x % 2)),
        y * 4 + (3 - x),
        (y + 1 - 2 * (y % 2)) * 4 + x,
        (3 - y) * 4 + x,
    )
    partner = p + 1 - 2 * core
    up, down = (p + 2) % PIPE, (p + PIPE - 2) % PIPE

    def local(src, dst, sem):
        return pltpu.make_async_copy(src, dst, sem)

    def send(src, dst, ssem, rsem, to_p, to_d):
        pltpu.make_async_remote_copy(
            src_ref=src, dst_ref=dst, send_sem=ssem, recv_sem=rsem,
            device_id=(to_p, to_d), device_id_type=MESH,
        ).start()

    def await_bytes(ref, sem):
        pltpu.make_async_copy(ref, ref, sem).wait()

    def rows(c, n=TC):
        return pl.ds(c * n, n)

    gin_l = [local(gin.at[0, rows(c)], gin_v.at[rows(c)], load_sem.at[c]) for c in range(C)]
    wout_l = local(wout.at[0, 0], wout_v, load_sem.at[3])
    x_l = local(saved.at[0, 0], x_v, load_sem.at[4])
    win_l = local(win.at[0, 0], win_v, load_sem.at[5])
    enc_l = local(enc, enc_v, load_sem.at[6])
    dec_l = local(dec, dec_v, load_sem.at[7])
    for copy in (wout_l, *gin_l, x_l, win_l, enc_l, dec_l):
        copy.start()

    barrier = pltpu.get_barrier_semaphore()

    def greet(k, _):
        pl.semaphore_signal(barrier, inc=1, device_id=(p, (d + k) % DP), device_id_type=MESH)
        return 0

    lax.fori_loop(1, DP, greet, 0)
    for by in (1, 2, PIPE - 2, PIPE - 1):
        pl.semaphore_signal(barrier, inc=1, device_id=((p + by) % PIPE, d), device_id_type=MESH)

    offs = []
    for q in range(Q):
        o = [0]
        for s in range(4):
            o.append(o[-1] + bits[(q + s) % 4] * (128 >> s))
        offs.append(o)

    def at(c, off, n):
        return pl.ds(pl.multiple_of(c * TC + off, n), n)

    def dh_partial(c):
        for q in range(Q):
            dhp[q, rows(c)] = dot(gin_v[rows(c)], wout_v[:, q * QW : (q + 1) * QW]).astype(BF)

    def dh_send(c):
        for q in range(Q):
            b = q % 4
            send(dhp.at[q, at(c, (1 - bits[b]) * 128, 128)], r0.at[c, q],
                 rs_send.at[c, 0], rs_recv.at[c, 0], p, peers[b])

    def step_bytes(c, s):
        if s < 4:
            return (r0, r1, r2, r3)[s].at[c]
        return r0.at[c, :, pl.ds(0, TS << (s - 4))]

    def cols(q):
        return slice(q * QW, (q + 1) * QW)

    def exchange_step(c, s):
        await_bytes(step_bytes(c, s), rs_recv.at[c, s])
        if s == 7:
            return
        for q in range(Q):
            if s < 3:
                n = 64 >> s
                v = bits[(q + s + 1) % 4]
                peer = peers[(q + s + 1) % 4]
                give, keep = (pl.ds(pl.multiple_of(w * n, n), n) for w in (1 - v, v))
                if s == 0:
                    mine = offs[q][1]
                    dst = r1
                    s1[c, q] = (dhp[q, at(c, mine + (1 - v) * n, n)].astype(F32)
                                + r0[c, q, give].astype(F32)).astype(BF)
                    send(s1.at[c, q], r1.at[c, q], rs_send.at[c, 1], rs_recv.at[c, 1], p, peer)
                    k1[c, q] = dhp[q, at(c, mine + v * n, n)].astype(F32) + r0[c, q, keep].astype(F32)
                elif s == 1:
                    s2[c, q] = k1[c, q, give] + r1[c, q, give].astype(F32)
                    send(s2.at[c, q], r2.at[c, q], rs_send.at[c, 2], rs_recv.at[c, 2], p, peer)
                    k2[c, q] = k1[c, q, keep] + r1[c, q, keep].astype(F32)
                else:
                    s3[c, q] = k2[c, q, give] + r2[c, q, give]
                    send(s3.at[c, q], r3.at[c, q], rs_send.at[c, 3], rs_recv.at[c, 3], p, peer)
                    k3[c, q] = k2[c, q, keep] + r2[c, q, keep]
            else:
                b = (q + 6 - s) % 4
                n = TS << (s - 3)
                own = at(c, offs[q][7 - s], n)
                if s == 3:
                    dhf[own, cols(q)] = (k3[c, q] + r3[c, q]).astype(BF)
                send(dhf.at[own, cols(q)], dhf.at[own, cols(q)],
                     rs_send.at[c, s + 1], rs_recv.at[c, s + 1], p, peers[b])

    def to_group(src_of, dst_of, ssem, rsem):
        def one(k, _):
            j = (d + k) % DP
            send(src_of(j), dst_of(j), ssem, rsem, p, j)
            return 0

        lax.fori_loop(1, DP, one, 0)

    tn_hop = z + core * (8 - 2 * z)
    tn_next = (p + 2 - 4 * core + PIPE) % PIPE

    def tn_forward(k):
        blk = pl.ds(pl.multiple_of(core * HALF + k * BLK, BLK), BLK)
        await_bytes(tn.at[blk], tn_recv.at[k])

        @pl.when(tn_hop < 7)
        def _():
            send(tn.at[blk], tn.at[blk], tn_send.at[0], tn_recv.at[k], tn_next, d)

        send(tn.at[blk], tn.at[blk], tn_send.at[2], tnx_recv, partner, d)

    def tn_gap(g):
        k = g - TN_FIRST - 2 * (tn_hop - 1)

        @pl.when((z > 0) & (k >= 0) & (k < NB))
        def _():
            tn_forward(k)

    def tn_rest(g):
        def one(k, _):
            tn_forward(k)
            return 0

        @pl.when(z > 0)
        def _():
            lax.fori_loop(jnp.clip(g - TN_FIRST - 2 * (tn_hop - 1), 0, NB), NB, one, 0)
            await_bytes(tn.at[pl.ds(0, HALF)], tnx_recv)

        @pl.when(p == 1)
        def _():
            await_bytes(tn, tnx_recv)

    def gt_forward(k):
        blk = pl.ds(pl.multiple_of(k * BLK, BLK), BLK)
        await_bytes(gt.at[blk], gt_recv.at[k])

        @pl.when(z < 7)
        def _():
            send(gt.at[blk], gt.at[blk], gt_send.at[0], gt_recv.at[k], up, d)

        send(gt.at[blk], gt.at[blk], gt_send.at[1], gtx_recv.at[k // (TC // BLK)], partner, d)

    wout_l.wait()
    gin_l[0].wait()
    dh_partial(0)
    pl.semaphore_wait(barrier, DP - 1 + 4)
    dh_send(0)
    x_l.wait()
    for c in range(C):
        xf = x_v[rows(c)].astype(F32)
        sqb[d, :, c * TC : (c + 1) * TC] = row_total(xf * xf)
    to_group(lambda j: sqb.at[d], lambda j: sqb.at[d], sq_sem.at[0], sq_sem.at[1])
    for c in range(1, C):
        gin_l[c].wait()
        dh_partial(c)
        dh_send(c)
    await_bytes(sqb.at[pl.ds(0, DP - 1)], sq_sem.at[1])
    squares = jnp.sum(sqb[...], axis=0)
    scale = lax.rsqrt(squares / MODEL_WIDTH + 1e-05)
    for c in range(C):
        rcol[rows(c)] = as_columns(scale[:, c * TC : (c + 1) * TC])

    @pl.when(p == 0)
    def _():
        def one(b, _):
            blk = pl.ds(pl.multiple_of(b * BLK, BLK), BLK)
            r = rcol[blk]
            for j in range(W // 128):
                js = slice(j * 128, (j + 1) * 128)
                tn[blk, js] = (x_v[blk, js].astype(F32) * r * tgain[:, js].astype(F32)).astype(BF)
            return 0

        def both(b, _):
            for stream in (0, 1):
                k = b + stream * NB
                one(k, 0)
                blk = pl.ds(pl.multiple_of(k * BLK, BLK), BLK)
                send(tn.at[blk], tn.at[blk], tn_send.at[stream], tn_recv.at[b],
                     up if stream == 0 else PIPE - 1, d)
            return 0

        lax.fori_loop(0, NB, both, 0)
        send(tn, tn, tn_send.at[2], tnx_recv, partner, d)

    win_l.wait()

    def back(c):
        lanes = jnp.zeros((1, TC), F32)
        for j in range(W // 256):
            js = slice(j * 256, (j + 1) * 256)
            u = dot(dhf[rows(c)], win_v[js, :], ((1,), (1,))) * gains[:, js].astype(F32)
            uf[rows(c), js] = u
            lanes = lanes + row_total(u * x_v[rows(c), js].astype(F32))
        ipb[c, d] = lanes
        to_group(lambda j: ipb.at[c, d], lambda j: ipb.at[c, d], ip_send.at[c], ip_recv.at[c])

    def finish(c):
        await_bytes(ipb.at[c, pl.ds(0, DP - 1)], ip_recv.at[c])
        inner = as_columns(jnp.sum(ipb[c], axis=0))
        r = rcol[rows(c)]
        coef = r * r * r * inner * (1.0 / MODEL_WIDTH)
        for j in range(W // 128):
            js = slice(j * 128, (j + 1) * 128)
            v = (gin_v[rows(c), js].astype(F32) + r * uf[rows(c), js]
                 - x_v[rows(c), js].astype(F32) * coef).astype(BF)
            dx[rows(c), js] = v

        @pl.when(p == 1)
        def _():
            gt[rows(c)] = dx[rows(c)]

            def one(i, _):
                k = c * (TC // BLK) + i
                blk = pl.ds(pl.multiple_of(k * BLK, BLK), BLK)
                send(dx.at[blk], gt.at[blk], gt_send.at[0], gt_recv.at[k], up, d)
                return 0

            lax.fori_loop(0, TC // BLK, one, 0)
            send(dx.at[rows(c)], gt.at[rows(c)], gt_send.at[1], gtx_recv.at[c], partner, d)

        send(dx.at[rows(c)], gout.at[0, rows(c)], go_send.at[c], go_recv.at[c],
             (p + PIPE - 1) % PIPE, d)

    g = 0
    for tau in range(8 + 2 * (C - 1) + 1):
        for c in range(C):
            s = tau - 2 * c
            if s == 8:
                finish(c)
            elif 0 <= s < 8:
                exchange_step(c, s)
                if s == 7:
                    back(c)
            else:
                continue
            tn_gap(g)
            g += 1
    tn_rest(g)

    def shard(c):
        return pl.ds(pl.multiple_of(c * TC + d * TS, TS), TS)

    def scatter(kind, c, a, b, dims):
        part[kind, rows(c)] = dot(a, b, dims).astype(BF)
        to_group(
            lambda j: part.at[kind, pl.ds(pl.multiple_of(c * TC + j * TS, TS), TS)],
            lambda j: rsb.at[kind, c, d], tr_send.at[2 * kind, c], tr_recv.at[2 * kind, c])
        rsb[kind, c, d] = part[kind, shard(c)]

    def total(kind, c):
        await_bytes(rsb.at[kind, c, pl.ds(0, DP - 1)], tr_recv.at[2 * kind, c])
        return jnp.sum(rsb[kind, c].astype(F32), axis=0)

    def gather(kind, c, values):
        full[kind, shard(c)] = values.astype(BF)
        to_group(
            lambda j: full.at[kind, shard(c)], lambda j: full.at[kind, shard(c)],
            tr_send.at[2 * kind + 1, c], tr_recv.at[2 * kind + 1, c])

    def gathered(kind, c):
        await_bytes(rsb.at[kind, c, pl.ds(0, DP - 1)], tr_recv.at[2 * kind + 1, c])

    enc_l.wait()
    for c in range(C):
        scatter(0, c, tn[rows(c)], enc_v[...], ((1,), (0,)))
    for c in range(C):
        v = total(0, c) + bias[...]
        tps[c] = v
        gather(0, c, 0.5 * v * (1.0 + jnp.tanh(GELU_A * (v + GELU_B * v * v * v))))
    dec_l.wait()
    for c in range(C):
        @pl.when((core == 1) & (z > 0))
        def _():
            def one(k, _):
                gt_forward(k)
                return 0

            lax.fori_loop(c * (TC // BLK), (c + 1) * (TC // BLK), one, 0)

        @pl.when(core == 0)
        def _():
            await_bytes(gt.at[rows(c)], gtx_recv.at[c])

        scatter(1, c, gt[rows(c)], dec_v[...], ((1,), (1,)))
    for c in range(C):
        v = tps[c]
        th = jnp.tanh(GELU_A * (v + GELU_B * v * v * v))
        slope = 0.5 * (1.0 + th) + 0.5 * v * (1.0 - th * th) * GELU_A * (1.0 + 3.0 * GELU_B * v * v)
        gather(1, c, total(1, c) * slope)
    for c in range(C):
        gathered(0, c)
    for j in range(W // 256):
        js = slice(j * 256, (j + 1) * 256)
        gd_v[:, js] = dot(full[0], gt[:, js], ((0,), (0,)))
    gd_out = local(gd_v, gdec, out_sem.at[0])
    gd_out.start()
    for c in range(C):
        gathered(1, c)
    for j in range(W // 256):
        js = slice(j * 256, (j + 1) * 256)
        ge_v[js, :] = dot(tn[:, js], full[1], ((0,), (0,)))
    ge_out = local(ge_v, genc, out_sem.at[1])
    ge_out.start()
    gbias[...] = jnp.sum(full[1].astype(F32), axis=0, keepdims=True)

    for c in range(C):
        await_bytes(dx.at[rows(c)], go_recv.at[c])
        await_bytes(dx.at[rows(c)], go_send.at[c])
        for s in range(8):
            await_bytes(step_bytes(c, s), rs_send.at[c, s])
        await_bytes(ipb.at[c, pl.ds(0, DP - 1)], ip_send.at[c])
        for kind in range(4):
            await_bytes(rsb.at[0, c, pl.ds(0, DP - 1)], tr_send.at[kind, c])
    await_bytes(sqb.at[pl.ds(0, DP - 1)], sq_sem.at[0])

    @pl.when(p == 0)
    def _():
        await_bytes(tn.at[pl.ds(0, HALF)], tn_send.at[0])
        await_bytes(tn.at[pl.ds(0, HALF)], tn_send.at[1])
        await_bytes(tn, tn_send.at[2])

    @pl.when(z > 0)
    def _():
        @pl.when(tn_hop < 7)
        def _():
            await_bytes(tn.at[pl.ds(0, HALF)], tn_send.at[0])

        await_bytes(tn.at[pl.ds(0, HALF)], tn_send.at[2])

    @pl.when(core == 1)
    def _():
        @pl.when(z < 7)
        def _():
            await_bytes(gt, gt_send.at[0])

        await_bytes(gt, gt_send.at[1])

    gd_out.wait()
    ge_out.wait()


def body(saved, grads_in, gains, w_in, w_out_t, encoder, enc_bias, decoder, transcoder_norm_gain):
    vmem = pl.BlockSpec(memory_space=pltpu.VMEM)
    anywhere = pl.BlockSpec(memory_space=pl.ANY)
    V = pltpu.VMEM
    DMA = pltpu.SemaphoreType.DMA
    scratch = [
        V((T, W), BF), V((T, W), BF), V((W, H), BF), V((W, H), BF), V((W, L), BF), V((L, W), BF),
        V((Q, T, QW), BF),
        V((C, Q, 128, QW), BF), V((C, Q, 64, QW), BF), V((C, Q, 32, QW), F32), V((C, Q, 16, QW), F32),
        V((C, Q, 64, QW), BF), V((C, Q, 64, QW), F32),
        V((C, Q, 32, QW), F32), V((C, Q, 32, QW), F32),
        V((C, Q, 16, QW), F32), V((C, Q, 16, QW), F32),
        V((T, H), BF), V((T, W), F32), V((T, W), BF), V((T, W), BF), V((T, W), BF),
        V((DP, 1, T), F32), V((C, DP, 1, TC), F32), V((T, 128), F32),
        V((2, T, L), BF), V((2, C, DP, TS, L), BF), V((C, TS, L), F32), V((2, T, L), BF),
        V((W, L), F32), V((L, W), F32),
        DMA((8,)), DMA((C, 8)), DMA((C, 8)), DMA((2,)), DMA((C,)), DMA((C,)), DMA((4, C)), DMA((4, C)),
        DMA((NB,)), DMA((3,)), DMA, DMA((2 * NB,)), DMA((2,)), DMA((C,)), DMA((C,)), DMA((C,)), DMA((2,)),
    ]
    gout, genc, gdec, gbias = pl.pallas_call(
        kernel,
        out_shape=(
            jax.ShapeDtypeStruct((1, T, W), BF),
            jax.ShapeDtypeStruct((W, L), F32),
            jax.ShapeDtypeStruct((L, W), F32),
            jax.ShapeDtypeStruct((1, L), F32),
        ),
        in_specs=[vmem] * 3 + [anywhere] * 6,
        out_specs=(anywhere, anywhere, anywhere, vmem),
        scratch_shapes=scratch,
        compiler_params=pltpu.CompilerParams(
            collective_id=0, has_side_effects=True, vmem_limit_bytes=56 * 1024 * 1024
        ),
        cost_estimate=pl.CostEstimate(flops=5_000_000_000, bytes_accessed=14_000_000, transcendentals=0),
    )(
        gains[0], enc_bias[None], transcoder_norm_gain[None],
        saved, grads_in, w_in, w_out_t, encoder, decoder,
    )
    return gout, genc, gdec, gbias[0]


def solution(mesh):
    in_specs = (
        P("pipe", None, None, "dp"),
        P("pipe", None, "dp"),
        P("pipe", None, "dp"),
        P("pipe", None, "dp", None),
        P("pipe", None, "dp", None),
        P("dp", "pipe"),
        P("pipe"),
        P("pipe", "dp"),
        P("dp"),
    )
    out_specs = (P("pipe", None, "dp"), P("dp", "pipe"), P("pipe", "dp"), P("pipe"))
    return jax.shard_map(body, mesh=mesh, in_specs=in_specs, out_specs=out_specs, check_vma=False)
```

time: 423 us -> 126 us (0.30)
  the two profiles are of different devices: /device:TPU:65 before, /device:TPU:224 now
where the time goes in v1:
time: 126 us
  Pallas kernels  118 us (94%)
  local copies, waits for them, and re-layouts  7.18 us (6%)
    pallas_call x1, Pallas kernels, body(): pl.pallas_call(kernel, out_shape=(jax.ShapeDtypeStruct((1, T, W), BF), ja...  118 us
    unnamed x10, local copies, waits for them, and re-layouts  5.9 us

profile of v1, /device:TPU:224, one launch (start us, length us, event | category | flops | bytes accessed | tf_op | source)
XLA Modules:
  0.0 125.6 jit_solution(1573388795369039988)
XLA Ops:
  0.6 1.3 %broadcast_in_dim.7.tgain = bf16[1,1024]{1,0:T(2,128)(2,1)} reshape(bf16[1024]{0:T(1024)(128)(2,1)} %param.17) | data formatting | bytes 4096 | tf_op jit(solution)/shard_map/broadcast_in_dim | solution.py:447
  1.9 117.8 %shard_map.120 = (bf16[1,768,1024]{2,1,0:T(8,128)(2,1)}, f32[1024,256]{1,0:T(8,128)}, f32[256,1024]{1,0:T(8,128)}, f32[1,256]{1,0:T(1,128)}) custom-call(bf16[1,1024]{1,0:T(2,128)(2,1)} %bitcast.4, f32[1,256]{1,0:T(1,128)} %bitcast.5, bf16[1,1024]{1,0:T(2,128)(2,1)} %broadcast_in_dim.7.tgain, bf16[1,1,768,1024]{3,2,1,0:T(8,128)(2,1)} %saved.1, ...), custom_call_target="tpu_custom_call" | custom-call | flops 5000000000 | bytes 14000000 | tf_op jit(solution)/shard_map/pallas_call | solution.py:431
  119.7 0.0 copy-start.1
  119.7 2.8 %copy.17 = bf16[1,768,1024]{2,1,0:T(8,128)(2,1)} copy(bf16[1,768,1024]{2,1,0:T(8,128)(2,1)} %get-tuple-element.16) | data formatting | bytes 3145728
  122.5 0.0 copy-done.1
  122.5 0.0 copy-start
  122.5 1.0 copy.18
  123.4 0.6 copy-done
  124.1 0.0 copy-start.2
  124.1 1.0 copy.19
  125.1 0.0 copy-done.2
  125.1 0.6 copy.20
Async XLA Ops:
  119.7 2.8 %copy-start.1 = (f32[1024,256]{1,0:T(8,128)S(1)}, f32[1024,256]{1,0:T(8,128)}, u32[]{:S(2)}) copy-start(f32[1024,256]{1,0:T(8,128)} %get-tuple-element.17) | copy-start | bytes 3145732
  122.5 1.6 %copy-start = (f32[256,1024]{1,0:T(8,128)S(1)}, f32[256,1024]{1,0:T(8,128)}, u32[]{:S(2)}) copy-start(f32[256,1024]{1,0:T(8,128)} %get-tuple-element.18) | copy-start | bytes 3145732
  124.1 1.0 copy-start.2

commit v2 on v1

v2 whole, which is shorter than its diff:
```python
import functools

import jax
import jax.numpy as jnp
from jax import lax
from jax.experimental import pallas as pl
from jax.experimental.pallas import tpu as pltpu
from jax.sharding import PartitionSpec as P

MESH = pl.DeviceIdType.MESH
BF = jnp.bfloat16
F32 = jnp.float32
MODEL_WIDTH = 16384
T, W, H, L = 768, 1024, 1024, 256
C, TC = 3, 256
HW = H // 2
XR, YR = TC // 4, TC // 16
DP, PIPE = 16, 16
TS = TC // DP
BLK = 32
HALF = T // 2
NB = HALF // BLK
GB = 32
GN = TC // GB
X0_AT = {"00": 8, "10": 10, "01": 14, "20": 16, "11": 18, "02": 20, "21": 22, "12": 24, "22": 64}
GT_LAG = 3
GT_AT = {"13": 3, "0f": 5, "23": 8, "1f": 11, "2f": 14}
GO_AFTER = "00"
Z_UP = 4
GELU_A = 0.7978845608028654
GELU_B = 0.044715


def dot(a, b, dims=((1,), (0,))):
    return lax.dot_general(a, b, (dims, ((), ())), preferred_element_type=F32)


def row_total(block):
    lanes = block[:, 0:128]
    for j in range(1, block.shape[1] // 128):
        lanes = lanes + block[:, j * 128 : (j + 1) * 128]
    return jnp.sum(lanes.T, axis=0, keepdims=True)


def as_columns(row):
    return jnp.broadcast_to(row, (128, row.shape[1])).T


def kernel(
    gains, bias, tgain, saved, gin, win, wout, enc, dec,
    gout, genc, gdec, gbias,
    x_v, gin_v, win_v, wout_v, enc_v, dec_v,
    dhp, p1r, p2s, p2r, dhf, uf, dx, x0, tn, gt, r0,
    sqb, ipb, rcol, part, rsb, tps, full, ge_v, gd_v,
    load_sem, rs_send, rs_recv, sq_sem, ip_send, ip_recv, tr_send, tr_recv,
    tn_recv, tn_send, tnx_recv, gt_recv, gt_send, gtx_recv, go_send, go_recv, out_sem, r0_sem, turn,
):
    p = lax.axis_index("pipe")
    d = lax.axis_index("dp")
    z, core = p // 2, p % 2
    y, x = d // 4, d % 4
    partner = p + 1 - 2 * core
    up, down = (p + 2) % PIPE, (p + PIPE - 2) % PIPE
    first = core == jnp.where(z == 0, 1, 0)
    carries_x0, carries_gt = (core == 1) & (z > 0), (core == 0) & (z > 0)

    def local(src, dst, sem):
        return pltpu.make_async_copy(src, dst, sem)

    def send(src, dst, ssem, rsem, to_p, to_d):
        pltpu.make_async_remote_copy(
            src_ref=src, dst_ref=dst, send_sem=ssem, recv_sem=rsem,
            device_id=(to_p, to_d), device_id_type=MESH,
        ).start()

    def await_bytes(ref, sem):
        pltpu.make_async_copy(ref, ref, sem).wait()

    def rows(c, n=TC):
        return pl.ds(c * n, n)

    gin_l = [local(gin.at[0, rows(c)], gin_v.at[rows(c)], load_sem.at[c]) for c in range(C)]
    wout_l = local(wout.at[0, 0], wout_v, load_sem.at[3])
    x_l = local(saved.at[0, 0], x_v, load_sem.at[4])
    win_l = local(win.at[0, 0], win_v, load_sem.at[5])
    enc_l = local(enc, enc_v, load_sem.at[6])
    dec_l = local(dec, dec_v, load_sem.at[7])
    for copy in (wout_l, *gin_l, x_l, win_l, enc_l, dec_l):
        copy.start()

    barrier = pltpu.get_barrier_semaphore()

    def greet(k, _):
        pl.semaphore_signal(barrier, inc=1, device_id=(p, (d + k) % DP), device_id_type=MESH)
        return 0

    lax.fori_loop(1, DP, greet, 0)
    for by in (1, 2, PIPE - 2, PIPE - 1):
        pl.semaphore_signal(barrier, inc=1, device_id=((p + by) % PIPE, d), device_id_type=MESH)

    @pl.when((p > 2) & (p < PIPE - 2))
    def _():
        pl.semaphore_signal(barrier, inc=1, device_id=(0, d), device_id_type=MESH)

    @pl.when(p == PIPE - 2)
    def _():
        pl.semaphore_signal(barrier, inc=1, device_id=(1, d), device_id_type=MESH)


    place = ((x, y), (y, x))

    def peer(h, axis, k):
        to = (place[h][axis] + k) % 4
        return (y * 4 + to if h == axis else to * 4 + x), to

    def some(start, n):
        return pl.ds(pl.multiple_of(start, n), n)

    def cols(h):
        return slice(h * HW, (h + 1) * HW)

    def dh_partial(c):
        for j in range(H // 256):
            js = slice((j % 2) * 256, (j % 2 + 1) * 256)
            dhp[j // 2, rows(c), js] = dot(gin_v[rows(c)], wout_v[:, j * 256 : (j + 1) * 256]).astype(BF)

    def dh_send():
        def one(c, _):
            for k in (1, 2, 3):
                for h in (0, 1):
                    j, to = peer(h, 0, k)
                    send(dhp.at[h, some(c * TC + to * XR, XR)], p1r.at[c, h, k - 1],
                         rs_send.at[c, 0], rs_recv.at[c, 0], p, j)
            return 0

        lax.fori_loop(0, C, one, 0)

    def step_bytes(c, s):
        return (p1r.at[c], p2r.at[c], p1r.at[c, :, :, pl.ds(0, YR)], p1r.at[c])[s]

    def exchange_step(c, s):
        await_bytes(step_bytes(c, s), rs_recv.at[c, s])
        for h in (0, 1):
            i, j = place[h]
            mine = c * TC + i * XR
            if s == 0:
                v = dhp[h, some(mine, XR)].astype(F32)
                for k in range(3):
                    v = v + p1r[c, h, k].astype(F32)
                p2s[c, h] = v
            elif s == 1:
                v = p2s[c, h, some(j * YR, YR)]
                for k in range(3):
                    v = v + p2r[c, h, k]
                dhf[some(mine + j * YR, YR), cols(h)] = v.astype(BF)
            for k in (1, 2, 3):
                if s == 0:
                    to_d, to = peer(h, 1, k)
                    send(p2s.at[c, h, some(to * YR, YR)], p2r.at[c, h, k - 1],
                         rs_send.at[c, 1], rs_recv.at[c, 1], p, to_d)
                elif s < 3:
                    own = some(mine + j * YR, YR) if s == 1 else some(mine, XR)
                    to_d, _ = peer(h, 1 if s == 1 else 0, k)
                    send(dhf.at[own, cols(h)], dhf.at[own, cols(h)],
                         rs_send.at[c, s + 1], rs_recv.at[c, s + 1], p, to_d)

    def to_group(src_of, dst_of, ssem, rsem):
        def one(k, _):
            j = (d + k) % DP
            send(src_of(j), dst_of(j), ssem, rsem, p, j)
            return 0

        lax.fori_loop(1, DP, one, 0)

    def x0_forward(stream, k):
        blk = pl.ds(pl.multiple_of(stream * HALF + k * BLK, BLK), BLK)
        sem = tn_recv.at[stream * NB + k]
        await_bytes(x0.at[blk], sem)

        @pl.when(z < 7 if stream == 0 else z > 1)
        def _():
            send(x0.at[blk], x0.at[blk], tn_send.at[stream], sem, (up, down)[stream], d)

        send(x0.at[blk], x0.at[blk], tn_send.at[2], tnx_recv, partner, d)

    def x0_done(stream, m):
        hops = z - 1 if stream == 0 else 7 - z
        return jnp.clip(m - 3 * hops, 0, NB)

    def x0_blocks(lo, hi):
        @pl.when(carries_x0)
        def _():
            for stream in (0, 1):
                def one(k, _, stream=stream):
                    x0_forward(stream, k)
                    return 0

                lax.fori_loop(x0_done(stream, lo), x0_done(stream, hi), one, 0)

    def tnorm():
        @pl.when((p == 1) | carries_gt)
        def _():
            await_bytes(x0, tnx_recv)

        @pl.when(p > 0)
        def _():
            await_bytes(r0, r0_sem.at[1])

        tg = tgain[...].astype(F32)[None, :]
        for c in range(C):
            r = as_columns(r0[:, c * TC : (c + 1) * TC])
            for j in range(W // 128):
                js = slice(j * 128, (j + 1) * 128)
                tn[rows(c), js] = (x0[rows(c), js].astype(F32) * r * tg[:, js]).astype(BF)

    goes_up = z <= Z_UP
    gt_hop = jnp.where(goes_up, z, 8 - z)
    gt_last = (z == Z_UP) | (z == Z_UP + 1)
    gt_next = jnp.where(goes_up, up, down)
    gt_root_down = Z_UP < 7

    def gt_forward(k):
        blk = pl.ds(pl.multiple_of(k * GB, GB), GB)
        await_bytes(gt.at[blk], gt_recv.at[k])

        @pl.when(jnp.logical_not(gt_last))
        def _():
            send(gt.at[blk], gt.at[blk], gt_send.at[0], gt_recv.at[k], gt_next, d)

        send(gt.at[blk], gt.at[blk], gt_send.at[1], gtx_recv.at[k // GN], partner, d)

    def gt_done(m):
        return jnp.clip(m - GT_LAG * (gt_hop - 1), 0, C * GN)

    def gt_blocks(lo, hi):
        def one(k, _):
            gt_forward(k)
            return 0

        @pl.when(carries_gt)
        def _():
            lax.fori_loop(lo, hi, one, 0)

    wout_l.wait()
    for c in range(C):
        gin_l[c].wait()
        dh_partial(c)
    pl.semaphore_wait(barrier, jnp.where(p == 0, DP + PIPE - 2, DP - 1 + 4 + jnp.where(p == 1, 1, 0)))
    pl.when(first)(dh_send)
    x_l.wait()

    @pl.when(p == 0)
    def _():
        x0[...] = x_v[...]

        def one(b, _):
            for stream in (0, 1):
                blk = pl.ds(pl.multiple_of(stream * HALF + b * BLK, BLK), BLK)
                send(x_v.at[blk], x0.at[blk], tn_send.at[stream], tn_recv.at[stream * NB + b],
                     3 if stream == 0 else PIPE - 1, d)
            return 0

        lax.fori_loop(0, NB, one, 0)
        send(x_v, x0, tn_send.at[2], tnx_recv, partner, d)

    for c in range(C):
        xf = x_v[rows(c)].astype(F32)
        sqb[d, :, c * TC : (c + 1) * TC] = row_total(xf * xf)
    to_group(lambda j: sqb.at[d], lambda j: sqb.at[d], sq_sem.at[0], sq_sem.at[1])

    def scale_ready():
        await_bytes(sqb.at[pl.ds(0, DP - 1)], sq_sem.at[1])
        squares = jnp.sum(sqb[...], axis=0)
        scale = lax.rsqrt(squares / MODEL_WIDTH + 1e-05)
        for c in range(C):
            rcol[rows(c)] = as_columns(scale[:, c * TC : (c + 1) * TC])

    @pl.when(p == 0)
    def _():
        scale_ready()
        squares = jnp.sum(sqb[...], axis=0)
        r0[...] = lax.rsqrt(squares / MODEL_WIDTH + 1e-05)

        def one(k, _):
            send(r0, r0, r0_sem.at[0], r0_sem.at[1], k, d)
            return 0

        lax.fori_loop(1, PIPE, one, 0)

    @pl.when(jnp.logical_not(first))
    def _():
        pl.semaphore_wait(turn, 1)
        dh_send()

    win_l.wait()
    enc_l.wait()
    dec_l.wait()

    def back(c):
        lanes = jnp.zeros((1, TC), F32)
        for j in range(W // 256):
            js = slice(j * 256, (j + 1) * 256)
            u = dot(dhf[rows(c)], win_v[js, :], ((1,), (1,))) * gains[:, js].astype(F32)
            uf[rows(c), js] = u
            lanes = lanes + row_total(u * x_v[rows(c), js].astype(F32))
        ipb[c, d] = lanes
        to_group(lambda j: ipb.at[c, d], lambda j: ipb.at[c, d], ip_send.at[c], ip_recv.at[c])

    dx_late = carries_gt & (z > Z_UP + 1)

    def pass_dx(c):
        send(dx.at[rows(c)], gout.at[0, rows(c)], go_send.at[c], go_recv.at[c],
             (p + PIPE - 1) % PIPE, d)

    def finish(c):
        await_bytes(ipb.at[c, pl.ds(0, DP - 1)], ip_recv.at[c])
        inner = as_columns(jnp.sum(ipb[c], axis=0))
        r = rcol[rows(c)]
        coef = r * r * r * inner * (1.0 / MODEL_WIDTH)
        for j in range(W // 128):
            js = slice(j * 128, (j + 1) * 128)
            v = (gin_v[rows(c), js].astype(F32) + r * uf[rows(c), js]
                 - x_v[rows(c), js].astype(F32) * coef).astype(BF)
            dx[rows(c), js] = v

        @pl.when(p == 1)
        def _():
            gt[rows(c)] = dx[rows(c)]

            def one(k, _):
                blk = pl.ds(pl.multiple_of(k * GB, GB), GB)
                send(dx.at[blk], gt.at[blk], gt_send.at[0], gt_recv.at[k], 2, d)
                if gt_root_down:
                    send(dx.at[blk], gt.at[blk], gt_send.at[2], gt_recv.at[k], PIPE - 2, d)
                return 0

            lax.fori_loop(c * GN, (c + 1) * GN, one, 0)
            send(dx.at[rows(c)], gt.at[rows(c)], gt_send.at[1], gtx_recv.at[c], partner, d)

        pl.when(jnp.logical_not(dx_late))(lambda: pass_dx(c))

    def shard(c):
        return pl.ds(pl.multiple_of(c * TC + d * TS, TS), TS)

    def scatter(kind, c, a, b, dims):
        part[kind, rows(c)] = dot(a, b, dims).astype(BF)
        to_group(
            lambda j: part.at[kind, pl.ds(pl.multiple_of(c * TC + j * TS, TS), TS)],
            lambda j: rsb.at[kind, c, d], tr_send.at[2 * kind, c], tr_recv.at[2 * kind, c])
        rsb[kind, c, d] = part[kind, shard(c)]

    def total(kind, c):
        await_bytes(rsb.at[kind, c, pl.ds(0, DP - 1)], tr_recv.at[2 * kind, c])
        return jnp.sum(rsb[kind, c].astype(F32), axis=0)

    def gather(kind, c, values):
        full[kind, shard(c)] = values.astype(BF)
        to_group(
            lambda j: full.at[kind, shard(c)], lambda j: full.at[kind, shard(c)],
            tr_send.at[2 * kind + 1, c], tr_recv.at[2 * kind + 1, c])

    def gathered(kind, c):
        await_bytes(rsb.at[kind, c, pl.ds(0, DP - 1)], tr_recv.at[2 * kind + 1, c])

    def tpre_partial():
        tnorm()
        for c in range(C):
            scatter(0, c, tn[rows(c)], enc_v[...], ((1,), (0,)))

    early_tnorm = carries_x0 | (p == 0)
    order = ("00", "10", "01", "20", "11", "02", "21", "12", "22", "03", "13", "0f", "23", "1f", "2f")
    gt_now = 0
    x0_now = 0
    for step in order:
        c = int(step[0])
        if step in X0_AT:
            x0_blocks(x0_now, X0_AT[step])
            x0_now = X0_AT[step]
        if step[1] == "f":
            finish(c)
        else:
            exchange_step(c, int(step[1]))
            if step[1] == "3":
                back(c)
            if step == GO_AFTER:
                @pl.when(first)
                def _():
                    pl.semaphore_signal(turn, inc=1, device_id=(partner, d), device_id_type=MESH)
        if step == "12":
            pl.when(p > 0)(scale_ready)
        if step == "22":
            pl.when(early_tnorm)(tpre_partial)
        if step in GT_AT:
            gt_blocks(gt_done(gt_now), gt_done(GT_AT[step]))
            gt_now = GT_AT[step]

    def gt_chunk(c):
        if c < C - 1:
            gt_blocks(jnp.clip(gt_done(gt_now), c * GN, (c + 1) * GN), (c + 1) * GN)

        @pl.when(carries_x0 | (p == 0))
        def _():
            await_bytes(gt.at[rows(c)], gtx_recv.at[c])

        scatter(1, c, gt[rows(c)], dec_v[...], ((1,), (1,)))

    def tpre_total():
        for c in range(C):
            v = total(0, c) + bias[...]
            tps[c] = v
            gather(0, c, 0.5 * v * (1.0 + jnp.tanh(GELU_A * (v + GELU_B * v * v * v))))

    def dtpre(c):
        v = tps[c]
        th = jnp.tanh(GELU_A * (v + GELU_B * v * v * v))
        slope = 0.5 * (1.0 + th) + 0.5 * v * (1.0 - th * th) * GELU_A * (1.0 + 3.0 * GELU_B * v * v)
        gather(1, c, total(1, c) * slope)

    far = carries_gt & (gt_hop >= 3)
    near = jnp.logical_not(far | early_tnorm)
    pl.when(early_tnorm)(tpre_total)
    gt_chunk(0)
    pl.when(far)(tpre_partial)
    gt_chunk(1)

    @pl.when(far)
    def _():
        tpre_total()
        dtpre(0)

    gt_blocks(jnp.clip(gt_done(gt_now), 2 * GN, C * GN), C * GN)

    @pl.when(dx_late)
    def _():
        for c in range(C):
            pass_dx(c)

    pl.when(near)(tpre_partial)
    gt_chunk(2)
    pl.when(near)(tpre_total)
    pl.when(jnp.logical_not(far))(lambda: dtpre(0))
    dtpre(1)
    dtpre(2)
    for c in range(C):
        gathered(0, c)
    for j in range(W // 256):
        js = slice(j * 256, (j + 1) * 256)
        gd_v[:, js] = dot(full[0], gt[:, js], ((0,), (0,)))
    gd_out = local(gd_v, gdec, out_sem.at[0])
    gd_out.start()
    for c in range(C):
        gathered(1, c)
    for j in range(W // 256):
        js = slice(j * 256, (j + 1) * 256)
        ge_v[js, :] = dot(tn[:, js], full[1], ((0,), (0,)))
    ge_out = local(ge_v, genc, out_sem.at[1])
    ge_out.start()
    gbias[...] = jnp.sum(full[1].astype(F32), axis=0, keepdims=True)

    for c in range(C):
        await_bytes(dx.at[rows(c)], go_recv.at[c])
        await_bytes(dx.at[rows(c)], go_send.at[c])
        for s in range(4):
            await_bytes(step_bytes(c, s), rs_send.at[c, s])
        await_bytes(ipb.at[c, pl.ds(0, DP - 1)], ip_send.at[c])
        for kind in range(4):
            await_bytes(rsb.at[0, c, pl.ds(0, DP - 1)], tr_send.at[kind, c])
    await_bytes(sqb.at[pl.ds(0, DP - 1)], sq_sem.at[0])

    @pl.when(p == 0)
    def _():
        await_bytes(tn.at[pl.ds(0, HALF)], tn_send.at[0])
        await_bytes(tn.at[pl.ds(0, HALF)], tn_send.at[1])
        await_bytes(tn, tn_send.at[2])

        await_bytes(sqb.at[pl.ds(0, PIPE - 1)], r0_sem.at[0])

    @pl.when(carries_x0)
    def _():
        @pl.when(z < 7)
        def _():
            await_bytes(tn.at[pl.ds(0, HALF)], tn_send.at[0])

        @pl.when(z > 1)
        def _():
            await_bytes(tn.at[pl.ds(0, HALF)], tn_send.at[1])

        await_bytes(tn, tn_send.at[2])

    @pl.when((p == 1) | (carries_gt & jnp.logical_not(gt_last)))
    def _():
        await_bytes(gt, gt_send.at[0])

    @pl.when((p == 1) | carries_gt)
    def _():
        await_bytes(gt, gt_send.at[1])

    if gt_root_down:
        @pl.when(p == 1)
        def _():
            await_bytes(gt, gt_send.at[2])

    gd_out.wait()
    ge_out.wait()


def body(saved, grads_in, gains, w_in, w_out_t, encoder, enc_bias, decoder, transcoder_norm_gain):
    vmem = pl.BlockSpec(memory_space=pltpu.VMEM)
    anywhere = pl.BlockSpec(memory_space=pl.ANY)
    V = pltpu.VMEM
    DMA = pltpu.SemaphoreType.DMA
    scratch = [
        V((T, W), BF), V((T, W), BF), V((W, H), BF), V((W, H), BF), V((W, L), BF), V((L, W), BF),
        V((2, T, HW), BF), V((C, 2, 3, XR, HW), BF), V((C, 2, XR, HW), F32), V((C, 2, 3, YR, HW), F32),
        V((T, H), BF), V((T, W), F32), V((T, W), BF), V((T, W), BF), V((T, W), BF), V((T, W), BF), V((1, T), F32),
        V((DP, 1, T), F32), V((C, DP, 1, TC), F32), V((T, 128), F32),
        V((2, T, L), BF), V((2, C, DP, TS, L), BF), V((C, TS, L), F32), V((2, T, L), BF),
        V((W, L), F32), V((L, W), F32),
        DMA((8,)), DMA((C, 4)), DMA((C, 4)), DMA((2,)), DMA((C,)), DMA((C,)), DMA((4, C)), DMA((4, C)),
        DMA((2 * NB,)), DMA((3,)), DMA, DMA((C * GN,)), DMA((3,)), DMA((C,)), DMA((C,)), DMA((C,)), DMA((2,)), DMA((2,)),
        pltpu.SemaphoreType.REGULAR,
    ]
    gout, genc, gdec, gbias = pl.pallas_call(
        kernel,
        out_shape=(
            jax.ShapeDtypeStruct((1, T, W), BF),
            jax.ShapeDtypeStruct((W, L), F32),
            jax.ShapeDtypeStruct((L, W), F32),
            jax.ShapeDtypeStruct((1, L), F32),
        ),
        in_specs=[vmem] * 3 + [anywhere] * 6,
        out_specs=(anywhere, anywhere, anywhere, vmem),
        scratch_shapes=scratch,
        compiler_params=pltpu.CompilerParams(
            collective_id=0, has_side_effects=True, vmem_limit_bytes=56 * 1024 * 1024
        ),
        cost_estimate=pl.CostEstimate(flops=5_000_000_000, bytes_accessed=14_000_000, transcendentals=0),
    )(
        gains[0], enc_bias[None], transcoder_norm_gain,
        saved, grads_in, w_in, w_out_t, encoder, decoder,
    )
    return gout, genc, gdec, gbias[0]


def solution(mesh):
    in_specs = (
        P("pipe", None, None, "dp"),
        P("pipe", None, "dp"),
        P("pipe", None, "dp"),
        P("pipe", None, "dp", None),
        P("pipe", None, "dp", None),
        P("dp", "pipe"),
        P("pipe"),
        P("pipe", "dp"),
        P("dp"),
    )
    out_specs = (P("pipe", None, "dp"), P("dp", "pipe"), P("pipe", "dp"), P("pipe"))
    return jax.shard_map(body, mesh=mesh, in_specs=in_specs, out_specs=out_specs, check_vma=False)
```

time: 126 us -> 83.3 us (0.66)
  the two profiles are of different devices: /device:TPU:224 before, /device:TPU:65 now
where the time goes in v2:
time: 83.3 us; the launch traced here: 81.8 us
  Pallas kernels  75.2 us (90%)
  local copies, waits for them, and re-layouts  5.9 us (7%)
    pallas_call x1, Pallas kernels, body(): pl.pallas_call(kernel, out_shape=(jax.ShapeDtypeStruct((1, T, W), BF), ja...  75.2 us
    unnamed x10, local copies, waits for them, and re-layouts  5.9 us

profile of v2, /device:TPU:65, one launch (start us, length us, event | category | flops | bytes accessed | tf_op | source)
XLA Modules:
  0.0 81.8 jit_solution(16768435053400935447)
XLA Ops:
  0.6 75.2 %shard_map.120 = (bf16[1,768,1024]{2,1,0:T(8,128)(2,1)}, f32[1024,256]{1,0:T(8,128)}, f32[256,1024]{1,0:T(8,128)}, f32[1,256]{1,0:T(1,128)}) custom-call(bf16[1,1024]{1,0:T(2,128)(2,1)} %bitcast.4, f32[1,256]{1,0:T(1,128)} %bitcast.5, bf16[1024]{0:T(1024)(128)(2,1)} %tgain.1, bf16[1,1,768,1024]{3,2,1,0:T(8,128)(2,1)} %saved.1, bf16[1,768,1024]{2,1,0:T(8,128)(2,1)} %gin.1, ...), custom_call_target="tpu_custom_call" | custom-call | flops 5000000000 | bytes 14000000 | tf_op jit(solution)/shard_map/pallas_call | solution.py:523
  75.9 0.0 copy-start.1
  75.9 2.8 %copy.17 = bf16[1,768,1024]{2,1,0:T(8,128)(2,1)} copy(bf16[1,768,1024]{2,1,0:T(8,128)(2,1)} %get-tuple-element.16) | data formatting | bytes 3145728
  78.6 0.0 copy-done.1
  78.7 0.0 copy-start
  78.7 1.0 %copy.18 = f32[1024,256]{1,0:T(8,128)} copy(f32[1024,256]{1,0:T(8,128)S(1)} %copy-done.1) | data formatting | bytes 2097152
  79.6 0.6 copy-done
  80.3 0.0 copy-start.2
  80.3 1.0 %copy.19 = f32[256,1024]{1,0:T(8,128)} copy(f32[256,1024]{1,0:T(8,128)S(1)} %copy-done) | data formatting | bytes 2097152
  81.2 0.0 copy-done.2
  81.2 0.6 copy.20
Async XLA Ops:
  75.9 2.8 %copy-start.1 = (f32[1024,256]{1,0:T(8,128)S(1)}, f32[1024,256]{1,0:T(8,128)}, u32[]{:S(2)}) copy-start(f32[1024,256]{1,0:T(8,128)} %get-tuple-element.17) | copy-start | bytes 3145732
  78.7 1.6 %copy-start = (f32[256,1024]{1,0:T(8,128)S(1)}, f32[256,1024]{1,0:T(8,128)}, u32[]{:S(2)}) copy-start(f32[256,1024]{1,0:T(8,128)} %get-tuple-element.18) | copy-start | bytes 3145732
  80.3 1.0 %copy-start.2 = (f32[1,256]{1,0:T(1,128)S(1)}, f32[1,256]{1,0:T(1,128)}, u32[]{:S(2)}) copy-start(f32[1,256]{1,0:T(1,128)} %get-tuple-element.11) | copy-start | bytes 3076

commit v3 on v2

--- a/solution.py
+++ b/solution.py
@@ -177,15 +177,15 @@
         sem = tn_recv.at[stream * NB + k]
         await_bytes(x0.at[blk], sem)
 
-        @pl.when(z < 7 if stream == 0 else z > 1)
+        @pl.when(z < 6 if stream == 0 else z > 2)
         def _():
             send(x0.at[blk], x0.at[blk], tn_send.at[stream], sem, (up, down)[stream], d)
 
         send(x0.at[blk], x0.at[blk], tn_send.at[2], tnx_recv, partner, d)
 
     def x0_done(stream, m):
-        hops = z - 1 if stream == 0 else 7 - z
-        return jnp.clip(m - 3 * hops, 0, NB)
+        late = jnp.where(z == 7, NB, 3 * z - 3) if stream == 0 else jnp.where(z == 1, NB, 21 - 3 * z)
+        return jnp.clip(m - late, 0, NB)
 
     def x0_blocks(lo, hi):
         @pl.when(carries_x0)
@@ -254,13 +254,13 @@
         x0[...] = x_v[...]
 
         def one(b, _):
-            for stream in (0, 1):
-                blk = pl.ds(pl.multiple_of(stream * HALF + b * BLK, BLK), BLK)
-                send(x_v.at[blk], x0.at[blk], tn_send.at[stream], tn_recv.at[stream * NB + b],
-                     3 if stream == 0 else PIPE - 1, d)
+            for way in (0, 1):
+                k = lax.rem(b + way * NB, 2 * NB)
+                blk = pl.ds(pl.multiple_of(k * BLK, BLK), BLK)
+                send(x_v.at[blk], x0.at[blk], tn_send.at[way], tn_recv.at[k], (3, PIPE - 1)[way], d)
             return 0
 
-        lax.fori_loop(0, NB, one, 0)
+        lax.fori_loop(0, 2 * NB, one, 0)
         send(x_v, x0, tn_send.at[2], tnx_recv, partner, d)
 
     for c in range(C):
@@ -469,19 +469,18 @@
 
     @pl.when(p == 0)
     def _():
-        await_bytes(tn.at[pl.ds(0, HALF)], tn_send.at[0])
-        await_bytes(tn.at[pl.ds(0, HALF)], tn_send.at[1])
-        await_bytes(tn, tn_send.at[2])
+        for way in range(3):
+            await_bytes(tn, tn_send.at[way])
 
         await_bytes(sqb.at[pl.ds(0, PIPE - 1)], r0_sem.at[0])
 
     @pl.when(carries_x0)
     def _():
-        @pl.when(z < 7)
+        @pl.when(z < 6)
         def _():
             await_bytes(tn.at[pl.ds(0, HALF)], tn_send.at[0])
 
-        @pl.when(z > 1)
+        @pl.when(z > 2)
         def _():
             await_bytes(tn.at[pl.ds(0, HALF)], tn_send.at[1])
 
@@ -502,6 +501,16 @@
 
     gd_out.wait()
     ge_out.wait()
+
+
+PARTS = 2
+
+
+def hand_over(gout, genc, gdec, gbias, gout_o, genc_o, gdec_o, gbias_o):
+    gout_o[...] = gout[...]
+    genc_o[...] = genc[...]
+    gdec_o[...] = gdec[...]
+    gbias_o[...] = gbias[...]
 
 
 def body(saved, grads_in, gains, w_in, w_out_t, encoder, enc_bias, decoder, transcoder_norm_gain):
@@ -539,6 +548,20 @@
         gains[0], enc_bias[None], transcoder_norm_gain,
         saved, grads_in, w_in, w_out_t, encoder, decoder,
     )
+    results = (gout, genc, gdec, gbias)
+    blocks = [
+        pl.BlockSpec((1, T // PARTS, W), lambda k: (0, k, 0)),
+        pl.BlockSpec((W // PARTS, L), lambda k: (k, 0)),
+        pl.BlockSpec((L // PARTS, W), lambda k: (k, 0)),
+        pl.BlockSpec((1, L), lambda k: (0, 0)),
+    ]
+    gout, genc, gdec, gbias = pl.pallas_call(
+        hand_over,
+        grid=(PARTS,),
+        out_shape=tuple(jax.ShapeDtypeStruct(a.shape, a.dtype) for a in results),
+        in_specs=blocks,
+        out_specs=tuple(blocks),
+    )(*results)
     return gout, genc, gdec, gbias[0]
 
 

time: 83.3 us -> 79.6 us (0.956); the launches traced: 81.8 us -> 79.5 us
  local copies, waits for them, and re-layouts: 5.9 us -> 0 us
  Pallas kernels: 75.2 us -> 78.9 us
    unnamed x10 -> x0, local copies, waits for them, and re-layouts: 5.9 us -> none
    pallas_call x0 -> x1, Pallas kernels: none -> 3.58 us  [body(): pl.pallas_call(hand_over, grid=(PARTS,), out_shape=tuple((jax.ShapeDtypeS...]
where the time goes in v3:
time: 79.6 us; the launch traced here: 79.5 us
  Pallas kernels  78.9 us (99%)
    pallas_call x1, Pallas kernels, body(): pl.pallas_call(kernel, out_shape=(jax.ShapeDtypeStruct((1, T, W), BF), ja...  75.3 us
    pallas_call x1, Pallas kernels, body(): pl.pallas_call(hand_over, grid=(PARTS,), out_shape=tuple((jax.ShapeDtypeS...  3.58 us

profile of v3, /device:TPU:65, one launch (start us, length us, event | category | flops | bytes accessed | tf_op | source)
XLA Modules:
  0.0 79.5 jit_solution(16453279982473903036)
XLA Ops:
  0.6 75.3 %shard_map.120 = (bf16[1,768,1024]{2,1,0:T(8,128)(2,1)}, f32[1024,256]{1,0:T(8,128)}, f32[256,1024]{1,0:T(8,128)}, f32[1,256]{1,0:T(1,128)}) custom-call(bf16[1,1024]{1,0:T(2,128)(2,1)} %bitcast.3, f32[1,256]{1,0:T(1,128)} %bitcast.4, bf16[1024]{0:T(1024)(128)(2,1)} %tgain.1, bf16[1,1,768,1024]{3,2,1,0:T(8,128)(2,1)} %saved.1, bf16[1,768,1024]{2,1,0:T(8,128)(2,1)} %gin.1, ...), custom_call_target="tpu_custom_call" | custom-call | flops 5000000000 | bytes 14000000 | tf_op jit(solution)/shard_map/pallas_call | solution.py:532
  75.9 3.6 %shard_map.121 = (bf16[1,768,1024]{2,1,0:T(8,128)(2,1)}, f32[1024,256]{1,0:T(8,128)}, f32[256,1024]{1,0:T(8,128)}, f32[1,256]{1,0:T(1,128)}) custom-call(bf16[1,768,1024]{2,1,0:T(8,128)(2,1)} %get-tuple-element.12.gout, f32[1024,256]{1,0:T(8,128)} %get-tuple-element.13.genc, f32[256,1024]{1,0:T(8,128)} %get-tuple-element.14.gdec, ...), custom_call_target="tpu_custom_call" | custom-call | tf_op jit(solution)/shard_map/pallas_call | solution.py:558

commit v4 on v3

--- a/solution.py
+++ b/solution.py
@@ -147,11 +147,11 @@
                 v = dhp[h, some(mine, XR)].astype(F32)
                 for k in range(3):
                     v = v + p1r[c, h, k].astype(F32)
-                p2s[c, h] = v
+                p2s[c, h] = v.astype(BF)
             elif s == 1:
-                v = p2s[c, h, some(j * YR, YR)]
+                v = p2s[c, h, some(j * YR, YR)].astype(F32)
                 for k in range(3):
-                    v = v + p2r[c, h, k]
+                    v = v + p2r[c, h, k].astype(F32)
                 dhf[some(mine + j * YR, YR), cols(h)] = v.astype(BF)
             for k in (1, 2, 3):
                 if s == 0:
@@ -448,11 +448,13 @@
         gd_v[:, js] = dot(full[0], gt[:, js], ((0,), (0,)))
     gd_out = local(gd_v, gdec, out_sem.at[0])
     gd_out.start()
-    for c in range(C):
-        gathered(1, c)
-    for j in range(W // 256):
-        js = slice(j * 256, (j + 1) * 256)
-        ge_v[js, :] = dot(tn[:, js], full[1], ((0,), (0,)))
+    for part_of, waits in ((slice(0, 2 * TC), (0, 1)), (slice(2 * TC, T), (2,))):
+        for c in waits:
+            gathered(1, c)
+        for j in range(W // 256):
+            js = slice(j * 256, (j + 1) * 256)
+            more = dot(tn[part_of, js], full[1, part_of], ((0,), (0,)))
+            ge_v[js, :] = more if waits[0] == 0 else ge_v[js, :] + more
     ge_out = local(ge_v, genc, out_sem.at[1])
     ge_out.start()
     gbias[...] = jnp.sum(full[1].astype(F32), axis=0, keepdims=True)
@@ -520,7 +522,7 @@
     DMA = pltpu.SemaphoreType.DMA
     scratch = [
         V((T, W), BF), V((T, W), BF), V((W, H), BF), V((W, H), BF), V((W, L), BF), V((L, W), BF),
-        V((2, T, HW), BF), V((C, 2, 3, XR, HW), BF), V((C, 2, XR, HW), F32), V((C, 2, 3, YR, HW), F32),
+        V((2, T, HW), BF), V((C, 2, 3, XR, HW), BF), V((C, 2, XR, HW), BF), V((C, 2, 3, YR, HW), BF),
         V((T, H), BF), V((T, W), F32), V((T, W), BF), V((T, W), BF), V((T, W), BF), V((T, W), BF), V((1, T), F32),
         V((DP, 1, T), F32), V((C, DP, 1, TC), F32), V((T, 128), F32),
         V((2, T, L), BF), V((2, C, DP, TS, L), BF), V((C, TS, L), F32), V((2, T, L), BF),

time: 79.6 us -> 78.5 us (0.986)
  Pallas kernels: 78.9 us -> 77.7 us
    pallas_call x1, Pallas kernels: 75.3 us -> 74.1 us  [body(): pl.pallas_call(kernel, out_shape=(jax.ShapeDtypeStruct((1, T, W), BF), ja...]
where the time goes in v4:
time: 78.5 us; the launch traced here: 78.4 us
  Pallas kernels  77.7 us (99%)
    pallas_call x1, Pallas kernels, body(): pl.pallas_call(kernel, out_shape=(jax.ShapeDtypeStruct((1, T, W), BF), ja...  74.1 us
    pallas_call x1, Pallas kernels, body(): pl.pallas_call(hand_over, grid=(PARTS,), out_shape=tuple((jax.ShapeDtypeS...  3.58 us

profile of v4, /device:TPU:65, one launch (start us, length us, event | category | flops | bytes accessed | tf_op | source)
XLA Modules:
  0.0 78.4 jit_solution(1043730944971067508)
XLA Ops:
  0.6 74.1 %shard_map.120 = (bf16[1,768,1024]{2,1,0:T(8,128)(2,1)}, f32[1024,256]{1,0:T(8,128)}, f32[256,1024]{1,0:T(8,128)}, f32[1,256]{1,0:T(1,128)}) custom-call(bf16[1,1024]{1,0:T(2,128)(2,1)} %bitcast.3, f32[1,256]{1,0:T(1,128)} %bitcast.4, bf16[1024]{0:T(1024)(128)(2,1)} %tgain.1, bf16[1,1,768,1024]{3,2,1,0:T(8,128)(2,1)} %saved.1, bf16[1,768,1024]{2,1,0:T(8,128)(2,1)} %gin.1, ...), custom_call_target="tpu_custom_call" | custom-call | flops 5000000000 | bytes 14000000 | tf_op jit(solution)/shard_map/pallas_call | solution.py:534
  74.8 3.6 %shard_map.121 = (bf16[1,768,1024]{2,1,0:T(8,128)(2,1)}, f32[1024,256]{1,0:T(8,128)}, f32[256,1024]{1,0:T(8,128)}, f32[1,256]{1,0:T(1,128)}) custom-call(bf16[1,768,1024]{2,1,0:T(8,128)(2,1)} %get-tuple-element.12.gout, f32[1024,256]{1,0:T(8,128)} %get-tuple-element.13.genc, f32[256,1024]{1,0:T(8,128)} %get-tuple-element.14.gdec, ...), custom_call_target="tpu_custom_call" | custom-call | tf_op jit(solution)/shard_map/pallas_call | solution.py:560
